TPU v7x, 32 devices: a whole 2x2x4 slice. The times are simulated.
32 devices in a mesh: dp: 8 (over y, x, core), fsdp: 4 (over z).
Axes of the slice: x: 2, y: 2, z: 4, core: 2. Of those that a mesh axis runs over, the one named last changes fastest.
Arguments:
- tokens: bfloat16 [16384, 1024], P(('dp', 'fsdp')), may hold values from -6 to 6
- segments: int32 [16384], P(('dp', 'fsdp')), may hold values from -1 to 1, as said below
- qkv_weight: bfloat16 [1024, 3072], P('fsdp'), may hold values from -6 to 6
- out_weight: bfloat16 [1024, 1024], P('fsdp'), may hold values from -0.1875 to 0.1875
Outputs:
- projected: bfloat16 [16384, 1024], P(('dp', 'fsdp'))
Inputs may be any that keep to these rules, and one draw needn't show every extreme that they name: `segments`: each image lies inside one block of 256 rows and is numbered 0 or 1 there; -1 marks empty rows. Each device's 512 rows begin with 0 to 2 blocks that hold images, its other blocks are empty. Two devices with equal fsdp index whose dp indices differ by half the dp axis hold 2 such blocks together; the first device holds 2.
All inputs are finite; a program needn't handle non-finite values.
Results may differ from a plain program's by a relative error of at most 0.0089.
Values may be sent and summed in bfloat16 or wider, within the bound.
A program may use at most 64 MiB of HBM per device.

v0:
```python
import jax
import jax.numpy as jnp
from jax import lax
from jax.sharding import PartitionSpec as P

HEADS = 16
BLK = 256


def normalize(block_rows):
    values_f = block_rows.astype(jnp.float32)
    row_mean = jnp.mean(values_f, axis=-1, keepdims=True)
    centered = values_f - row_mean
    variance = jnp.mean(centered * centered, axis=-1, keepdims=True)
    return (centered * lax.rsqrt(variance + 1e-05)).astype(jnp.bfloat16)


def attend(packed_qkv, segment, head_count):
    row_count = packed_qkv.shape[0]
    model_width = packed_qkv.shape[1] // 3
    head_dim = model_width // head_count
    queries = packed_qkv[:, :model_width].reshape(row_count, head_count, head_dim)
    key_rows = packed_qkv[:, model_width : 2 * model_width].reshape(row_count, head_count, head_dim)
    values = packed_qkv[:, 2 * model_width :].reshape(row_count, head_count, head_dim)
    scores = jnp.einsum(
        "qhd,khd->hqk", queries, key_rows, preferred_element_type=jnp.float32
    ) * head_dim ** (-0.5)
    same_image = segment[:, None] == segment[None, :]
    scores = jnp.where(same_image[None], scores, -1e30)
    row_max = jnp.max(scores, axis=-1, keepdims=True)
    weights = jnp.exp(scores - row_max)
    row_total = jnp.sum(weights, axis=-1, keepdims=True)
    attention = (weights / row_total).astype(jnp.bfloat16)
    mixed_rows = jnp.einsum("hqk,khd->qhd", attention, values, preferred_element_type=jnp.float32)
    return mixed_rows.reshape(row_count, model_width).astype(jnp.bfloat16)


def body(tokens, segments, qkv_weight, out_weight):
    row_count, model_width = tokens.shape
    block_count = row_count // BLK
    block_segments = segments.reshape(block_count, BLK)
    normed = normalize(tokens)
    columns = normed
    packed_qkv = jnp.dot(
        columns,
        lax.all_gather(qkv_weight, "fsdp", axis=0, tiled=True),
        preferred_element_type=jnp.float32,
    ).astype(jnp.bfloat16)
    mixed_blocks = lax.map(
        lambda operands: attend(operands[0], operands[1], HEADS),
        (packed_qkv.reshape(block_count, BLK, 3 * model_width), block_segments),
    )
    mixed_rows = mixed_blocks.reshape(row_count, model_width)
    columns = mixed_rows
    result = jnp.dot(
        columns,
        lax.all_gather(out_weight, "fsdp", axis=0, tiled=True),
        preferred_element_type=jnp.float32,
    )
    return jnp.where(segments[:, None] >= 0, result, 0.0).astype(jnp.bfloat16)


def solution(mesh):
    return jax.shard_map(
        body,
        mesh=mesh,
        in_specs=(P(("dp", "fsdp"), None), P(("dp", "fsdp")), P("fsdp", None), P("fsdp", None)),
        out_specs=P(("dp", "fsdp"), None),
        check_vma=False,
    )
```

profile of v0, /device:TPU:11, one launch (start us, length us, event | category | flops | bytes accessed | tf_op | source)
XLA Modules:
  0.0 180.3 jit_solution(4098586665417239850)
XLA Ops:
  6.5 0.0 copy-start.1
  6.5 0.0 copy-start
  6.5 0.0 all-gather.3.cloned.1.call-start
  6.5 0.7 all-gather.3.cloned.1.call-update
  7.3 0.0 all-gather.5.cloned.1.call-start
  7.3 0.7 all-gather.5.cloned.1.call-update
  8.0 0.0 copy-done.1
  8.1 0.0 copy-done
  8.1 0.2 convert_reduce_fusion
  8.3 0.4 fusion.13
  8.7 114.0 %all-gather.3.cloned.1.call-done = bf16[1024,3072]{1,0:T(8,128)(2,1)} async-done(((bf16[256,3072]{1,0:T(8,128)(2,1)}), bf16[1024,3072]{1,0:T(8,128)(2,1)}) %all-gather.3.cloned.1.call-update) | async-done | bytes 6291472 | tf_op jit(solution)/shard_map/all_gather | solution.py:46
  122.7 7.8 %convolution_convert_fusion = bf16[512,3072]{1,0:T(8,128)(2,1)} fusion(bf16[1024,3072]{1,0:T(8,128)(2,1)} %all-gather.3.cloned.1.call-done, bf16[512,1024]{1,0:T(8,128)(2,1)S(1)} %copy-done, f32[512]{0:T(512)S(1)} %add_rsqrt_fusion, f32[512]{0:T(512)S(1)} %broadcast_multiply_fusion), kind=kOutput, calls=%fused_computation.17 | convolution fusion | flops 3224895488 | bytes 10489856 | tf_op jit(solution)/shard_map/dot_general | solution.py:44
  130.5 20.0 %while.10 = (s32[]{:T(128)}, bf16[2,256,1024]{2,1,0:T(8,128)(2,1)}, bf16[2,256,3072]{2,1,0:T(8,128)(2,1)}, s32[2,256]{1,0:T(2,128)S(1)}, s32[]{:T(128)}) while((s32[]{:T(128)}, bf16[2,256,1024]{2,1,0:T(8,128)(2,1)}, bf16[2,256,3072]{2,1,0:T(8,128)(2,1)}, s32[2,256]{1,0:T(2,128)S(1)}, s32[]{:T(128)}) %tuple.34), condition=%wide.region_5.6_spmd, body=%wide.region_2.5_spmd.sunk | while | flops 275054848 | bytes 30575744 | solution.py:49
  130.5 1.5 constant_dynamic-slice_fusion.4
  132.1 0.7 copy.16
  132.8 0.1 fusion.37
  132.9 0.1 broadcast_compare_fusion.3
  133.0 3.4 %fusion.38 = (f32[16,256]{1,0:T(8,128)S(1)}, f32[16,256,256]{1,2,0:T(8,128)}) fusion(pred[256,256]{0,1:T(8,128)(4,1)S(1)} %broadcast_compare_fusion.3, bf16[256,16,64]{0,2,1:T(8,128)(2,1)S(1)} %bitcast.41, bf16[256,16,64]{0,2,1:T(8,128)(2,1)S(1)} %bitcast.40), kind=kOutput, calls=%fused_computation.31.clone.1 | convolution fusion | flops 138412288 | bytes 5324800 | tf_op jit(solution)/shard_map/while/body/eval_jaxpr/sub | solution.py:31
  136.4 0.0 copy-start.2
  136.4 2.8 %fusion.39 = bf16[16,64,256]{2,1,0:T(8,128)(2,1)S(1)} fusion(bf16[256,16,64]{0,2,1:T(8,128)(2,1)S(1)} %bitcast.39, f32[16,256,256]{1,2,0:T(8,128)} %get-tuple-element.82, f32[16,256]{1,0:T(8,128)S(1)} %get-tuple-element.83), kind=kOutput, calls=%fused_computation.9.clone.1 | convolution fusion | flops 136577024 | bytes 5259264 | tf_op jit(solution)/shard_map/while/body/eval_jaxpr/hqk,khd->qhd/dot_general | solution.py:34
  139.3 0.2 copy.17
  139.5 0.0 copy-done.2
  139.5 0.0 copy-start.3
  139.5 1.0 copy-done.3
  140.5 1.5 constant_dynamic-slice_fusion.4
  142.0 0.7 copy.16
  142.7 0.1 fusion.37
  142.9 0.1 broadcast_compare_fusion.3
  143.0 3.4 %fusion.38 = (f32[16,256]{1,0:T(8,128)S(1)}, f32[16,256,256]{1,2,0:T(8,128)}) fusion(pred[256,256]{0,1:T(8,128)(4,1)S(1)} %broadcast_compare_fusion.3, bf16[256,16,64]{0,2,1:T(8,128)(2,1)S(1)} %bitcast.41, bf16[256,16,64]{0,2,1:T(8,128)(2,1)S(1)} %bitcast.40), kind=kOutput, calls=%fused_computation.31.clone.1 | convolution fusion | flops 138412288 | bytes 5324800 | tf_op jit(solution)/shard_map/while/body/eval_jaxpr/sub | solution.py:31
  146.4 0.0 copy-start.2
  146.4 2.9 %fusion.39 = bf16[16,64,256]{2,1,0:T(8,128)(2,1)S(1)} fusion(bf16[256,16,64]{0,2,1:T(8,128)(2,1)S(1)} %bitcast.39, f32[16,256,256]{1,2,0:T(8,128)} %get-tuple-element.82, f32[16,256]{1,0:T(8,128)S(1)} %get-tuple-element.83), kind=kOutput, calls=%fused_computation.9.clone.1 | convolution fusion | flops 136577024 | bytes 5259264 | tf_op jit(solution)/shard_map/while/body/eval_jaxpr/hqk,khd->qhd/dot_general | solution.py:34
  149.3 0.2 copy.17
  149.5 0.0 copy-done.2
  149.6 0.0 copy-start.3
  149.6 1.0 copy-done.3
  150.5 18.8 %all-gather.5.cloned.1.call-done = bf16[1024,1024]{1,0:T(8,128)(2,1)} async-done(((bf16[256,1024]{1,0:T(8,128)(2,1)}), bf16[1024,1024]{1,0:T(8,128)(2,1)}) %all-gather.5.cloned.1.call-update) | async-done | bytes 2097168 | tf_op jit(solution)/shard_map/all_gather | solution.py:57
  169.4 4.1 %select_convert_fusion = bf16[512,1024]{1,0:T(8,128)(2,1)} fusion(bf16[512,1024]{1,0:T(8,128)(2,1)} %bitcast.43, bf16[1024,1024]{1,0:T(8,128)(2,1)} %all-gather.5.cloned.1.call-done, pred[512]{0:T(512)(128)(4,1)S(1)} %broadcast_compare_fusion.1), kind=kOutput, calls=%fused_computation.24 | convolution fusion | flops 1074790400 | bytes 4194816 | tf_op jit(solution)/shard_map/dot_general | solution.py:55
  (9 shorter events, 0.1 us)
Async XLA Ops:
  6.5 1.5 copy-start.1
  6.5 1.5 copy-start
  6.5 116.2 %all-gather.3.cloned.1.call-start = ((), (), s32[]{:S(2)}) async-start(), calls=%async_computation | async-start | bytes 7864320 | tf_op jit(solution)/shard_map/all_gather | solution.py:46
  7.3 162.1 %all-gather.5.cloned.1.call-start = ((), (), s32[]{:S(2)}) async-start(), calls=%async_computation.1 | async-start | bytes 2621440 | tf_op jit(solution)/shard_map/all_gather | solution.py:57
  136.4 3.0 %copy-start.2 = (bf16[2,256,1024]{2,1,0:T(8,128)(2,1)S(1)}, bf16[2,256,1024]{2,1,0:T(8,128)(2,1)}, u32[]{:S(2)}) copy-start(bf16[2,256,1024]{2,1,0:T(8,128)(2,1)} %get-tuple-element.90) | copy-start | bytes 3145732 | tf_op jit(solution)/shard_map/while
  139.5 1.0 copy-start.3
  146.4 3.1 %copy-start.2 = (bf16[2,256,1024]{2,1,0:T(8,128)(2,1)S(1)}, bf16[2,256,1024]{2,1,0:T(8,128)(2,1)}, u32[]{:S(2)}) copy-start(bf16[2,256,1024]{2,1,0:T(8,128)(2,1)} %get-tuple-element.90) | copy-start | bytes 3145732 | tf_op jit(solution)/shard_map/while
  149.6 1.0 copy-start.3
Sparse Core Ops, SparseCore 0:
  8.9 113.7 all-gather.2
  124.3 45.0 all-gather.4
where the time goes:
time: 184 us; the launch traced here: 180 us
  waiting for transfers between devices  134 us (73%)
  matrix products  24.5 us (13%)
  between operations  13.4 us (7%)
  local copies, waits for them, and re-layouts  7.1 us (4%)
    all_gather x1, waiting for transfers between devices, body(): lax.all_gather(qkv_weight, 'fsdp', axis=0, tiled=True)  114 us
    all_gather x1, waiting for transfers between devices, body(): lax.all_gather(out_weight, 'fsdp', axis=0, tiled=True)  18.8 us
    dot_general x1, matrix products, body(): jnp.dot(columns, lax.all_gather(qkv_weight, 'fsdp', axis=0, tiled=True),...  7.83 us
    sub x2, matrix products, attend(): weights = jnp.exp(scores - row_max)  6.89 us
    dot_general x2, matrix products, attend(): jnp.einsum('hqk,khd->qhd', attention, values, preferred_element_type=jnp....  5.67 us
    dynamic_slice x6, local copies, waits for them, and re-layouts, body(): lax.map(lambda operands: attend(operands[0], operands[1], HEADS), (packed...  4.43 us
    dot_general x1, matrix products, body(): jnp.dot(columns, lax.all_gather(out_weight, 'fsdp', axis=0, tiled=True),...  4.14 us
  transfers between devices with their start and end apart: 2, of which 2 were waited for; matrix products, arithmetic and copies ran while one was open for 15% of the time, Pallas kernels for 0%

commit v1 on v0

v1 whole, which is shorter than its diff:
```python
import functools
import math

import jax
import jax.numpy as jnp
from jax import lax
from jax.experimental import pallas as pl
from jax.experimental.pallas import tpu as pltpu
from jax.sharding import PartitionSpec as P

HEADS = 16
BLK = 256
LOG2E = math.log2(math.e)
MESH = pl.DeviceIdType.MESH


def rows_of(start, count):
    return pl.ds(pl.multiple_of(start, count), count)


def kernel(
    shards,
    tok_ref,
    seg_ref,
    qkv_ref,
    ow_ref,
    out_ref,
    wbuf,
    obuf,
    nbuf,
    segbuf,
    bias,
    sendbuf,
    mix,
    local_sem,
    z_send,
    z_recv,
    x_send,
    x_recv,
    y_send,
    y_recv,
    d_send,
    d_recv,
    o_send,
    o_recv,
    m_send,
    m_recv,
    t_send,
    t_recv,
):
    rows, width = tok_ref.shape
    head_dim = width // HEADS
    pair = 2 * head_dim
    half = width // 2
    groups = half // pair
    shard = qkv_ref.shape[0]
    quarter = shard // 4
    blocks = rows // BLK
    steps = range(1, shards)

    dp = lax.axis_index("dp")
    z = lax.axis_index("fsdp")
    core = lax.rem(dp, 2)
    x = lax.rem(dp // 2, 2)
    y = lax.rem(dp // 4, 2)
    x_dev = (dp + 2 - 4 * x, z)
    y_dev = (dp + 4 - 8 * y, z)
    c_dev = (dp + 1 - 2 * core, z)
    other = 1 - core
    part = 2 * y + x
    x_part = 2 * y + 1 - x
    y_part = 2 * (1 - y) + x
    d_part = 2 * (1 - y) + 1 - x

    def ahead(s):
        return lax.rem(z + s, shards)

    def behind(s):
        return lax.rem(z + shards - s, shards)

    def place(k, source, piece):
        where = rows_of(source * shard + piece * quarter, quarter)
        if k < groups:
            return wbuf.at[k, where, :]
        return obuf.at[core, where, :]

    def remote(ref, send, recv, device):
        return pltpu.make_async_remote_copy(
            src_ref=ref, dst_ref=ref, send_sem=send, recv_sem=recv, device_id=device, device_id_type=MESH
        )

    own = rows_of(z * shard, shard)
    local = []
    for k in range(groups):
        local.append(
            [
                pltpu.make_async_copy(
                    qkv_ref.at[:, pl.ds(pl.multiple_of(j * width + core * half + k * pair, pair), pair)],
                    wbuf.at[k, own, j * pair : (j + 1) * pair],
                    local_sem.at[3 * k + j],
                )
                for j in range(3)
            ]
        )
    local.append(
        [
            pltpu.make_async_copy(
                ow_ref.at[:, h * half : (h + 1) * half], obuf.at[h, own, :], local_sem.at[3 * groups + h]
            )
            for h in range(2)
        ]
    )
    for copies in local:
        for copy in copies:
            copy.start()

    barrier = pltpu.get_barrier_semaphore()
    for s in steps:
        pl.semaphore_signal(barrier, inc=1, device_id=(dp, ahead(s)), device_id_type=MESH)
    for device in (x_dev, y_dev, c_dev):
        pl.semaphore_signal(barrier, inc=1, device_id=device, device_id_type=MESH)
    pl.semaphore_wait(barrier, shards + 2)

    pending = []

    def start(copy):
        copy.start()
        pending.append(copy)

    def z_copy(k, s, source, device):
        return remote(place(k, source, part), z_send.at[k, s - 1], z_recv.at[k, s - 1], device)

    for k in range(groups + 1):
        for copy in local[k]:
            copy.wait()
        for s in steps:
            start(z_copy(k, s, z, (dp, ahead(s))))

    segbuf[core] = jnp.broadcast_to(seg_ref[...], segbuf.shape[1:])
    seg_copy = remote(segbuf.at[core], t_send.at[0], t_recv.at[0], c_dev)
    start(seg_copy)

    tile = 64

    @pl.loop(0, rows // tile)
    def _(i):
        where = rows_of(i * tile, tile)
        values = tok_ref[where, :].astype(jnp.float32)
        centered = values - jnp.mean(values, axis=-1, keepdims=True)
        variance = jnp.mean(centered * centered, axis=-1, keepdims=True)
        nbuf[core, where, :] = (centered * lax.rsqrt(variance + 1e-05)).astype(jnp.bfloat16)

    start(remote(nbuf.at[core], t_send.at[1], t_recv.at[1], c_dev))
    remote(segbuf.at[other], t_send.at[0], t_recv.at[0], c_dev).wait_recv()

    for c in range(2):
        for b in range(blocks):
            ids = segbuf[c, 0:1, b * BLK : (b + 1) * BLK].astype(jnp.float32)
            along = jnp.broadcast_to(ids, (BLK, BLK))
            bias[c, b] = jnp.where(along == along.T, 0.0, -1e30)

    def x_copy(k, s, piece):
        return remote(place(k, behind(s), piece), x_send.at[k, s - 1], x_recv.at[k, s - 1], x_dev)

    def y_copy(k, s, piece):
        return remote(place(k, behind(s), piece), y_send.at[k, s - 1], y_recv.at[k, s - 1], y_dev)

    def d_copy(k, s, piece, device):
        return remote(place(k, behind(s), piece), d_send.at[k, s - 1], d_recv.at[k, s - 1], device)

    def by_x(k, s):
        return (k + s) % 2 == 0

    def spread(k):
        for s in steps:
            z_copy(k, s, behind(s), (dp, ahead(s))).wait_recv()
            start(x_copy(k, s, part))
            start(y_copy(k, s, part))

    def cross(k):
        for s in steps:
            if by_x(k, s):
                x_copy(k, s, x_part).wait_recv()
                start(d_copy(k, s, x_part, y_dev))
            else:
                y_copy(k, s, y_part).wait_recv()
                start(d_copy(k, s, y_part, x_dev))

    def finish(k, s):
        if by_x(k, s):
            y_copy(k, s, y_part).wait_recv()
            d_copy(k, s, d_part, y_dev).wait_recv()
        else:
            x_copy(k, s, x_part).wait_recv()
            d_copy(k, s, d_part, x_dev).wait_recv()

    lane = lax.broadcasted_iota(jnp.int32, (BLK, pair), 1)
    first = lane < head_dim

    def attend(k, owner, b):
        where = rows_of(b * BLK, BLK)
        packed = jnp.dot(
            nbuf[owner, where, :], wbuf[k], preferred_element_type=jnp.float32
        ).astype(jnp.bfloat16)
        queries = packed[:, :pair]
        keys = packed[:, pair : 2 * pair]
        values = packed[:, 2 * pair :]
        zero = jnp.zeros_like(queries)
        one = jnp.ones_like(values)
        mixed = []
        for keep in (first, ~first):
            scores = lax.dot_general(
                jnp.where(keep, queries, zero), keys, (((1,), (1,)), ((), ())), preferred_element_type=jnp.float32
            )
            scores = scores * (LOG2E * head_dim ** (-0.5)) + bias[owner, b]
            weights = jnp.exp2(scores - jnp.max(scores, axis=-1, keepdims=True)).astype(jnp.bfloat16)
            mixed.append(
                jnp.dot(weights, jnp.where(keep, values, one), preferred_element_type=jnp.float32)
            )
        totals = pltpu.roll(jnp.where(first, mixed[1], mixed[0]), head_dim, 1)
        return (jnp.where(first, mixed[0], mixed[1]) / totals).astype(jnp.bfloat16)

    def m_copy(k, owner):
        return pltpu.make_async_remote_copy(
            src_ref=sendbuf.at[k],
            dst_ref=mix.at[owner * groups + k],
            send_sem=m_send.at[k],
            recv_sem=m_recv.at[k],
            device_id=c_dev,
            device_id_type=MESH,
        )

    def theirs(k):
        for s in steps:
            finish(k, s)

        @pl.loop(0, blocks)
        def _(b):
            sendbuf[k, rows_of(b * BLK, BLK), :] = attend(k, other, b)

        start(m_copy(k, core))

    def mine(k):
        @pl.loop(0, blocks)
        def _(b):
            mix[core * groups + k, rows_of(b * BLK, BLK), :] = attend(k, core, b)

    spread(0)
    spread(1)
    cross(0)
    spread(2)
    cross(1)
    remote(nbuf.at[other], t_send.at[1], t_recv.at[1], c_dev).wait_recv()
    for k in range(groups):
        theirs(k)
        if k + 3 <= groups:
            spread(k + 3)
        if k + 2 <= groups:
            cross(k + 2)
        mine(k)

    def o_copy(s, owner):
        where = rows_of(behind(s) * shard, shard)
        return remote(obuf.at[owner, where, :], o_send.at[s - 1], o_recv.at[s - 1], c_dev)

    for s in steps:
        finish(groups, s)
        start(o_copy(s, core))
    for k in range(groups):
        m_copy(k, other).wait_recv()

    def project(h):
        @pl.loop(0, blocks)
        def _(b):
            where = rows_of(b * BLK, BLK)
            mixed = jnp.concatenate([mix[j, where, :] for j in range(2 * groups)], axis=1)
            result = jnp.dot(mixed, obuf[h], preferred_element_type=jnp.float32)
            ids = jnp.broadcast_to(segbuf[core, 0:1, where].astype(jnp.float32), (pair, BLK)).T
            keep = jnp.concatenate([ids] * (half // pair), axis=1) >= 0.0
            out_ref[where, pl.ds(pl.multiple_of(h * half, half), half)] = jnp.where(keep, result, 0.0).astype(
                jnp.bfloat16
            )

    project(core)
    for s in steps:
        o_copy(s, other).wait_recv()
    project(other)
    for copy in pending:
        copy.wait_send()


def body(tokens, segments, qkv_weight, out_weight, shards):
    rows, width = tokens.shape
    half = width // 2
    pair = 2 * (width // HEADS)
    groups = half // pair
    blocks = rows // BLK
    vmem = pl.BlockSpec(memory_space=pltpu.VMEM)
    hbm = pl.BlockSpec(memory_space=pl.ANY)
    bf16 = jnp.bfloat16
    dma = pltpu.SemaphoreType.DMA
    sets = dma((groups + 1, shards - 1))
    return pl.pallas_call(
        functools.partial(kernel, shards),
        out_shape=jax.ShapeDtypeStruct((rows, width), bf16),
        in_specs=[vmem, vmem, hbm, hbm],
        out_specs=vmem,
        scratch_shapes=[
            pltpu.VMEM((groups, width, 3 * pair), bf16),
            pltpu.VMEM((2, width, half), bf16),
            pltpu.VMEM((2, rows, width), bf16),
            pltpu.VMEM((2, 8, rows), jnp.int32),
            pltpu.VMEM((2, blocks, BLK, BLK), jnp.float32),
            pltpu.VMEM((groups, rows, pair), bf16),
            pltpu.VMEM((2 * groups, rows, pair), bf16),
            dma((3 * groups + 2,)),
            *([sets] * 8),
            dma((shards - 1,)),
            dma((shards - 1,)),
            dma((groups,)),
            dma((groups,)),
            dma((2,)),
            dma((2,)),
        ],
        compiler_params=pltpu.CompilerParams(
            collective_id=0, has_side_effects=True, vmem_limit_bytes=48 * 1024 * 1024
        ),
    )(tokens, segments.reshape(1, rows), qkv_weight, out_weight)


def solution(mesh):
    return jax.shard_map(
        functools.partial(body, shards=mesh.shape["fsdp"]),
        mesh=mesh,
        in_specs=(P(("dp", "fsdp"), None), P(("dp", "fsdp")), P("fsdp", None), P("fsdp", None)),
        out_specs=P(("dp", "fsdp"), None),
        check_vma=False,
    )
```

time: 184 us -> 54 us (0.29); the launches traced: 180 us -> 53.8 us
  waiting for transfers between devices: 134 us -> 0 us
  Pallas kernels: 0 us -> 48.4 us
  matrix products: 24.5 us -> 0 us
  between operations: 13.4 us -> 0.01 us
    all_gather x2 -> x0, waiting for transfers between devices: 133 us -> none  [the longest x1 114 us: body(): lax.all_gather(qkv_weight, 'fsdp', axis=0, tiled=True)]
    pallas_call x0 -> x1, Pallas kernels: none -> 48.4 us  [body(): pl.pallas_call(functools.partial(kernel, shards), out_shape=jax.ShapeDtyp...]
    dot_general x4 -> x0, matrix products: 17.6 us -> none  [the longest x1 7.83 us: body(): jnp.dot(columns, lax.all_gather(qkv_weight, 'fsdp', axis=0, tiled=True),...]
    sub x2 -> x0, matrix products: 6.89 us -> none  [attend(): weights = jnp.exp(scores - row_max)]
    unnamed x4 -> x9, local copies, waits for them, and re-layouts: 0.01 us -> 5.33 us
    dynamic_slice x6 -> x0, local copies, waits for them, and re-layouts: 4.43 us -> none  [body(): lax.map(lambda operands: attend(operands[0], operands[1], HEADS), (packed...]
    while x8 -> x0, local copies, waits for them, and re-layouts: 1.93 us -> none
  transfers between devices with their start and end apart: 2 -> 0, of which waited for: 2 -> 0; matrix products, arithmetic and copies ran while one was open for 15% -> 0% of each run, Pallas kernels for 0% -> 0%
where the time goes in v1:
time: 54 us; the launch traced here: 53.8 us
  Pallas kernels  48.4 us (90%)
  local copies, waits for them, and re-layouts  5.33 us (10%)
    pallas_call x1, Pallas kernels, body(): pl.pallas_call(functools.partial(kernel, shards), out_shape=jax.ShapeDtyp...  48.4 us
    unnamed x9, local copies, waits for them, and re-layouts  5.33 us

profile of v1, /device:TPU:11, one launch (start us, length us, event | category | flops | bytes accessed | tf_op | source)
XLA Modules:
  0.0 53.8 jit_solution(11425646824130030125)
XLA Ops:
  0.0 0.0 copy-start
  0.0 1.4 %copy-done = bf16[256,3072]{1,0:T(8,128)(2,1)S(1)} copy-done((bf16[256,3072]{1,0:T(8,128)(2,1)S(1)}, bf16[256,3072]{1,0:T(8,128)(2,1)}, u32[]{:S(2)}) %copy-start) | copy-done | bytes 1572888
  1.4 0.0 copy-start.1
  1.4 1.2 %copy-done.1 = bf16[512,1024]{1,0:T(8,128)(2,1)S(1)} copy-done((bf16[512,1024]{1,0:T(8,128)(2,1)S(1)}, bf16[512,1024]{1,0:T(8,128)(2,1)}, u32[]{:S(2)}) %copy-start.1) | copy-done | bytes 1048600
  2.6 0.0 copy-start.2
  2.6 1.0 %copy-done.2 = bf16[256,1024]{1,0:T(8,128)(2,1)S(1)} copy-done((bf16[256,1024]{1,0:T(8,128)(2,1)S(1)}, bf16[256,1024]{1,0:T(8,128)(2,1)}, u32[]{:S(2)}) %copy-start.2) | copy-done | bytes 524312
  3.7 0.0 copy-start.3
  3.7 0.7 %copy-done.3 = s32[512]{0:T(512)S(1)} copy-done((s32[512]{0:T(512)S(1)}, s32[512]{0:T(512)}, u32[]{:S(2)}) %copy-start.3) | copy-done | bytes 2072
  4.4 48.4 %shard_map.46 = bf16[512,1024]{1,0:T(8,128)(2,1)S(1)} custom-call(bf16[512,1024]{1,0:T(8,128)(2,1)S(1)} %copy-done.1, s32[1,512]{1,0:T(1,128)S(1)} %bitcast.1, bf16[256,3072]{1,0:T(8,128)(2,1)S(1)} %copy-done, bf16[256,1024]{1,0:T(8,128)(2,1)S(1)} %copy-done.2), custom_call_target="tpu_custom_call" | custom-call | tf_op jit(solution)/shard_map/pallas_call | solution.py:303
  52.8 1.0 %copy.6 = bf16[512,1024]{1,0:T(8,128)(2,1)} copy(bf16[512,1024]{1,0:T(8,128)(2,1)S(1)} %shard_map.46) | data formatting | bytes 2097152
Async XLA Ops:
  0.0 1.4 %copy-start = (bf16[256,3072]{1,0:T(8,128)(2,1)S(1)}, bf16[256,3072]{1,0:T(8,128)(2,1)}, u32[]{:S(2)}) copy-start(bf16[256,3072]{1,0:T(8,128)(2,1)} %qkv_ref.1) | copy-start | bytes 4718596
  1.4 1.2 %copy-start.1 = (bf16[512,1024]{1,0:T(8,128)(2,1)S(1)}, bf16[512,1024]{1,0:T(8,128)(2,1)}, u32[]{:S(2)}) copy-start(bf16[512,1024]{1,0:T(8,128)(2,1)} %tok_ref.1) | copy-start | bytes 3145732
  2.6 1.0 %copy-start.2 = (bf16[256,1024]{1,0:T(8,128)(2,1)S(1)}, bf16[256,1024]{1,0:T(8,128)(2,1)}, u32[]{:S(2)}) copy-start(bf16[256,1024]{1,0:T(8,128)(2,1)} %ow_ref.1) | copy-start | bytes 1572868
  3.7 0.7 %copy-start.3 = (s32[512]{0:T(512)S(1)}, s32[512]{0:T(512)}, u32[]{:S(2)}) copy-start(s32[512]{0:T(512)} %param.5) | copy-start | bytes 6148

commit v2 on v1

--- a/solution.py
+++ b/solution.py
@@ -130,11 +130,15 @@
     def z_copy(k, s, source, device):
         return remote(place(k, source, part), z_send.at[k, s - 1], z_recv.at[k, s - 1], device)
 
-    for k in range(groups + 1):
-        for copy in local[k]:
-            copy.wait()
-        for s in steps:
-            start(z_copy(k, s, z, (dp, ahead(s))))
+    def launch(k):
+        if k <= groups:
+            for copy in local[k]:
+                copy.wait()
+            for s in steps:
+                start(z_copy(k, s, z, (dp, ahead(s))))
+
+    launch(0)
+    launch(1)
 
     segbuf[core] = jnp.broadcast_to(seg_ref[...], segbuf.shape[1:])
     seg_copy = remote(segbuf.at[core], t_send.at[0], t_recv.at[0], c_dev)
@@ -171,20 +175,27 @@
     def by_x(k, s):
         return (k + s) % 2 == 0
 
+    def spread_one(k, s):
+        z_copy(k, s, behind(s), (dp, ahead(s))).wait_recv()
+        start(x_copy(k, s, part))
+        start(y_copy(k, s, part))
+
+    def cross_one(k, s):
+        if by_x(k, s):
+            x_copy(k, s, x_part).wait_recv()
+            start(d_copy(k, s, x_part, y_dev))
+        else:
+            y_copy(k, s, y_part).wait_recv()
+            start(d_copy(k, s, y_part, x_dev))
+
     def spread(k):
-        for s in steps:
-            z_copy(k, s, behind(s), (dp, ahead(s))).wait_recv()
-            start(x_copy(k, s, part))
-            start(y_copy(k, s, part))
+        launch(k + 2)
+        for s in steps:
+            spread_one(k, s)
 
     def cross(k):
         for s in steps:
-            if by_x(k, s):
-                x_copy(k, s, x_part).wait_recv()
-                start(d_copy(k, s, x_part, y_dev))
-            else:
-                y_copy(k, s, y_part).wait_recv()
-                start(d_copy(k, s, y_part, x_dev))
+            cross_one(k, s)
 
     def finish(k, s):
         if by_x(k, s):
@@ -230,20 +241,21 @@
             device_id_type=MESH,
         )
 
-    def theirs(k):
+    def compute(k, duties):
         for s in steps:
             finish(k, s)
-
-        @pl.loop(0, blocks)
-        def _(b):
-            sendbuf[k, rows_of(b * BLK, BLK), :] = attend(k, other, b)
-
-        start(m_copy(k, core))
-
-    def mine(k):
-        @pl.loop(0, blocks)
-        def _(b):
-            mix[core * groups + k, rows_of(b * BLK, BLK), :] = attend(k, core, b)
+        turns = 2 * blocks
+        for turn in range(turns):
+            b = turn % blocks
+            where = slice(b * BLK, (b + 1) * BLK)
+            if turn < blocks:
+                sendbuf[k, where, :] = attend(k, other, b)
+            else:
+                mix[core * groups + k, where, :] = attend(k, core, b)
+            if turn == blocks - 1:
+                start(m_copy(k, core))
+            for duty in duties[turn * len(duties) // turns : (turn + 1) * len(duties) // turns]:
+                duty()
 
     spread(0)
     spread(1)
@@ -252,12 +264,14 @@
     cross(1)
     remote(nbuf.at[other], t_send.at[1], t_recv.at[1], c_dev).wait_recv()
     for k in range(groups):
-        theirs(k)
-        if k + 3 <= groups:
-            spread(k + 3)
-        if k + 2 <= groups:
-            cross(k + 2)
-        mine(k)
+        duties = []
+        for s in steps:
+            if k + 3 <= groups:
+                duties.append(functools.partial(spread_one, k + 3, s))
+        for s in steps:
+            if k + 2 <= groups:
+                duties.append(functools.partial(cross_one, k + 2, s))
+        compute(k, duties)
 
     def o_copy(s, owner):
         where = rows_of(behind(s) * shard, shard)
@@ -323,7 +337,7 @@
             dma((2,)),
         ],
         compiler_params=pltpu.CompilerParams(
-            collective_id=0, has_side_effects=True, vmem_limit_bytes=48 * 1024 * 1024
+            collective_id=0, has_side_effects=True, vmem_limit_bytes=63 << 20
         ),
     )(tokens, segments.reshape(1, rows), qkv_weight, out_weight)
 

time: 54 us -> 50.5 us (0.935)
  local copies, waits for them, and re-layouts: 5.33 us -> 2.26 us
    unnamed x9 -> x1, local copies, waits for them, and re-layouts: 5.33 us -> 2.26 us
where the time goes in v2:
time: 50.5 us; the launch traced here: 50.2 us
  Pallas kernels  47.9 us (95%)
  local copies, waits for them, and re-layouts  2.26 us (4%)
    pallas_call x1, Pallas kernels, body(): pl.pallas_call(functools.partial(kernel, shards), out_shape=jax.ShapeDtyp...  47.9 us
    unnamed x1, local copies, waits for them, and re-layouts  2.26 us

profile of v2, /device:TPU:11, one launch (start us, length us, event | category | flops | bytes accessed | tf_op | source)
XLA Modules:
  0.0 50.2 jit_solution(15674676111162122347)
XLA Ops:
  0.0 47.9 %shard_map.46 = bf16[512,1024]{1,0:T(8,128)(2,1)} custom-call(bf16[512,1024]{1,0:T(8,128)(2,1)} %tok_ref.1, s32[1,512]{1,0:T(1,128)} %bitcast.1, bf16[256,3072]{1,0:T(8,128)(2,1)} %qkv_ref.1, bf16[256,1024]{1,0:T(8,128)(2,1)} %ow_ref.1), custom_call_target="tpu_custom_call" | custom-call | tf_op jit(solution)/shard_map/pallas_call | solution.py:317
  47.9 2.3 %copy.6 = bf16[512,1024]{1,0:T(8,128)(2,1)} copy(bf16[512,1024]{1,0:T(8,128)(2,1)} %shard_map.46) | data formatting | bytes 2097152
